TPU v7x, 32 devices: a whole 2x2x4 slice. The times are simulated.
32 devices in a mesh: groups: 2 (over y), ctx: 16 (over z, x, core).
Axes of the slice: x: 2, y: 2, z: 4, core: 2. Of those that a mesh axis runs over, the one named last changes fastest.
Arguments:
- queries: bfloat16 [8192, 4096], P(('groups', 'ctx')), parts along dimension 0, may hold values from -13 to 13
- all_key_states: bfloat16 [8192, 512], P(('groups', 'ctx')), parts along dimension 0, may hold values from -9.5 to 9.5
- all_value_states: bfloat16 [8192, 512], P(('groups', 'ctx')), parts along dimension 0, may hold values from -6 to 6
- selected: int32 [32, 2], P(('groups', 'ctx')), parts along dimension 0, may hold values from 0 to 14, as said below
Outputs:
- attended: bfloat16 [8192, 4096], P(('groups', 'ctx')), parts along dimension 0
There are 2 independent parts, one for each index of `groups`. A program takes and returns all parts, laid end to end along the dimension named above; each array names one. Nothing has to cross between parts.
Inputs may be any that keep to these rules, and one draw needn't show every extreme that they name: `selected`: for block i >= 2 the two entries of row i are different blocks below i; rows 0 and 1 hold 0 and 0; the last block's first entry is 14.
All inputs are finite; a program needn't handle non-finite values.
Results may differ from a plain program's by a relative error of at most 0.004.
Values may be sent and summed in bfloat16 or wider, within the bound.
No kernel may reach another device: no remote copies, remote signals or barrier semaphores. Data moves between devices by JAX's collectives and lax.ppermute only.
A program may use at most 64 MiB of HBM per device.

v0:
```python
import math

import jax
import jax.numpy as jnp
from jax import lax
from jax.experimental import pallas as pl
from jax.experimental.pallas import tpu as pltpu
from jax.sharding import PartitionSpec as P

QUERY_HEADS = 32
KEY_VALUE_HEADS = 4
HEAD_SIZE = 128
GROUP = QUERY_HEADS // KEY_VALUE_HEADS
SLOTS = 2 * KEY_VALUE_HEADS
REQUEST_ROWS = 16
MIB = 1024 * 1024


def pack_kernel(selected_ref, key_ref, value_ref, out_ref):
    devices, piece_rows = out_ref.shape[0], key_ref.shape[0] // out_ref.shape[0]
    for slot in range(SLOTS):
        ref = key_ref if slot < KEY_VALUE_HEADS else value_ref
        head = slot % KEY_VALUE_HEADS
        part = ref[:, head * HEAD_SIZE : (head + 1) * HEAD_SIZE]
        out_ref[:, slot * piece_rows : (slot + 1) * piece_rows, :] = part.reshape(
            devices, piece_rows, HEAD_SIZE
        )
    lane = lax.broadcasted_iota(jnp.int32, (devices, REQUEST_ROWS, HEAD_SIZE), 2)
    request = jnp.where(lane == 0, selected_ref[0, 0], selected_ref[0, 1])
    out_ref[:, SLOTS * piece_rows :, :] = request.astype(jnp.float32).astype(jnp.bfloat16)


def pack(keys, values, selected, devices):
    rows = keys.shape[0]
    piece_rows = rows // devices
    shape = (devices, SLOTS * piece_rows + REQUEST_ROWS, HEAD_SIZE)
    if piece_rows % 16 == 0:
        return pl.pallas_call(
            pack_kernel,
            out_shape=jax.ShapeDtypeStruct(shape, jnp.bfloat16),
            in_specs=[
                pl.BlockSpec(memory_space=pltpu.SMEM),
                pl.BlockSpec(memory_space=pltpu.VMEM),
                pl.BlockSpec(memory_space=pltpu.VMEM),
            ],
            out_specs=pl.BlockSpec(memory_space=pltpu.VMEM),
            name="pack",
        )(selected, keys, values)
    both = jnp.concatenate([keys, values], axis=1)
    both = both.reshape(devices, piece_rows, SLOTS, HEAD_SIZE).transpose(0, 2, 1, 3)
    both = both.reshape(devices, SLOTS * piece_rows, HEAD_SIZE)
    lane = jnp.arange(HEAD_SIZE) == 0
    request = jnp.where(lane, selected[0, 0], selected[0, 1]).astype(jnp.bfloat16)
    request = jnp.broadcast_to(request, (devices, REQUEST_ROWS, HEAD_SIZE))
    return jnp.concatenate([both, request], axis=1)


def pick_kernel(wanted_ref, held_ref, out_ref):
    rows = out_ref.shape[2]

    @pl.loop(0, out_ref.shape[0])
    def _(device):
        for pick in range(2):
            out_ref[device, pick] = held_ref[wanted_ref[device, pick], :rows, :]


def pick_pieces(wanted, held):
    devices, rows = held.shape[0], held.shape[1] - REQUEST_ROWS
    return pl.pallas_call(
        pick_kernel,
        out_shape=jax.ShapeDtypeStruct((devices, 2, rows, HEAD_SIZE), jnp.bfloat16),
        in_specs=[
            pl.BlockSpec(memory_space=pltpu.SMEM),
            pl.BlockSpec(memory_space=pltpu.VMEM),
        ],
        out_specs=pl.BlockSpec(memory_space=pltpu.VMEM),
        compiler_params=pltpu.CompilerParams(vmem_limit_bytes=16 * MIB),
        name="pick_pieces",
    )(wanted, held)


HEADS_AT_ONCE = 4
FACTOR = math.log2(math.e) / math.sqrt(HEAD_SIZE)
LARGE_SUM = 2.0**100


def head_lanes(head):
    return slice(head * HEAD_SIZE, (head + 1) * HEAD_SIZE)


def with_ones(value):
    return jnp.concatenate([value, jnp.ones_like(value)], axis=1)


def inverse_of(positive):
    inverse = pl.reciprocal(positive, approx=True)
    return inverse * (2.0 - positive * inverse)


def stacked_queries(query_ref, first):
    heads = range(first, first + HEADS_AT_ONCE)
    return jnp.concatenate([query_ref[:, head_lanes(h)] for h in heads], axis=0)


def staggered(steps, score, finish):
    scores = score(steps[0])
    for step, later in zip(steps, steps[1:] + [None]):
        following = None if later is None else score(later)
        finish(step, scores)
        scores = following


STEPS = list(range(0, GROUP, HEADS_AT_ONCE))


def own_kernel(query_ref, key_ref, value_ref, out_ref, level_ref):
    rows = query_ref.shape[0]
    row = lax.broadcasted_iota(jnp.int32, (rows, rows), 0)
    column = lax.broadcasted_iota(jnp.int32, (rows, rows), 1)
    causal = column <= row
    lane = lax.broadcasted_iota(jnp.int32, (rows, HEAD_SIZE), 1)
    keys_across = key_ref[...].T
    value = with_ones(value_ref[...])

    def score(first):
        return jnp.dot(
            stacked_queries(query_ref, first), keys_across, preferred_element_type=jnp.float32
        )

    def finish(first, scores):
        weights, shifts = [], []
        for h in range(HEADS_AT_ONCE):
            part = jnp.where(causal, scores[h * rows : (h + 1) * rows], -1e30)
            shift = jnp.max(part, axis=1, keepdims=True) * FACTOR
            shifts.append(shift)
            weights.append(jnp.exp2(part * FACTOR - shift).astype(jnp.bfloat16))
        both = jnp.dot(
            jnp.concatenate(weights, axis=0), value, preferred_element_type=jnp.float32
        )
        for h in range(HEADS_AT_ONCE):
            part = both[h * rows : (h + 1) * rows]
            row_sum = part[:, HEAD_SIZE:]
            out_ref[:, head_lanes(first + h)] = part[:, :HEAD_SIZE] * inverse_of(row_sum)
            level = shifts[h] + jnp.log2(row_sum)
            level_ref[...] = jnp.where(lane == first + h, level, level_ref[...])

    level_ref[...] = jnp.zeros_like(level_ref)
    staggered(STEPS, score, finish)


def own_attention(queries, keys, values):
    rows = queries.shape[0]
    width = GROUP * HEAD_SIZE
    scores = QUERY_HEADS * rows * rows
    return pl.pallas_call(
        own_kernel,
        out_shape=[
            jax.ShapeDtypeStruct(queries.shape, jnp.float32),
            jax.ShapeDtypeStruct((rows, KEY_VALUE_HEADS * HEAD_SIZE), jnp.float32),
        ],
        grid=(KEY_VALUE_HEADS,),
        in_specs=[
            pl.BlockSpec((rows, width), lambda g: (0, g)),
            pl.BlockSpec((rows, HEAD_SIZE), lambda g: (0, g)),
            pl.BlockSpec((rows, HEAD_SIZE), lambda g: (0, g)),
        ],
        out_specs=[
            pl.BlockSpec((rows, width), lambda g: (0, g)),
            pl.BlockSpec((rows, HEAD_SIZE), lambda g: (0, g)),
        ],
        compiler_params=pltpu.CompilerParams(vmem_limit_bytes=24 * MIB),
        cost_estimate=pl.CostEstimate(
            flops=4 * scores * HEAD_SIZE, bytes_accessed=7 * MIB, transcendentals=scores
        ),
        name="own_attention",
    )(queries, keys, values)


def far_kernel(
    selected_ref, query_ref, far_ref, own_hbm, level_hbm, out_ref, own_ref, level_ref, staged, sems
):
    rows = query_ref.shape[0]
    width = GROUP * HEAD_SIZE

    def lanes(group, size):
        start = group * size
        return pl.ds(start if isinstance(group, int) else pl.multiple_of(start, size), size)

    def fetch(group):
        wide, narrow = lanes(group, width), lanes(group, HEAD_SIZE)
        return (
            pltpu.make_async_copy(own_hbm.at[:, wide], own_ref.at[group], sems.at[0, group]),
            pltpu.make_async_copy(level_hbm.at[:, narrow], level_ref.at[group], sems.at[1, group]),
        )

    def send(group):
        out = out_ref.at[:, lanes(group, width)]
        return pltpu.make_async_copy(staged.at[group], out, sems.at[2, group])

    for group in range(KEY_VALUE_HEADS):
        for copy in fetch(group):
            copy.start()

    def arrive(group):
        for copy in fetch(group):
            copy.wait()

    def block(slot, picks):
        blocks = [far_ref[:, p, slot].reshape(rows, HEAD_SIZE) for p in picks]
        return jnp.concatenate(blocks, axis=0)

    def keys_and_values(group, picks):
        return block(group, picks).T, with_ones(block(group + KEY_VALUE_HEADS, picks))

    def score(group, head, keys_across):
        query = stacked_queries(query_ref.at[:, lanes(group, width)], head)
        return jnp.dot(query, keys_across, preferred_element_type=jnp.float32)

    def quick(group, head, scores, value, largest):
        weights = []
        for h in range(HEADS_AT_ONCE):
            part = scores[h * rows : (h + 1) * rows]
            mine = level_ref[group, :, head + h : head + h + 1]
            weights.append(jnp.exp2(part * FACTOR - mine).astype(jnp.bfloat16))
        both = jnp.dot(
            jnp.concatenate(weights, axis=0), value, preferred_element_type=jnp.float32
        )
        for h in range(HEADS_AT_ONCE):
            part = both[h * rows : (h + 1) * rows]
            row_sum = 1.0 + part[:, HEAD_SIZE:]
            largest = jnp.maximum(
                largest, jnp.max(row_sum.reshape(rows // 8, 8, HEAD_SIZE), axis=0)
            )
            mixture = own_ref[group, :, head_lanes(head + h)] + part[:, :HEAD_SIZE]
            staged[group, :, head_lanes(head + h)] = (mixture * inverse_of(row_sum)).astype(
                staged.dtype
            )
        return largest

    def careful(group, head, scores, value):
        for h in range(HEADS_AT_ONCE):
            part = scores[h * rows : (h + 1) * rows] * FACTOR
            mine = level_ref[group, :, head + h : head + h + 1]
            shift = jnp.maximum(jnp.max(part, axis=1, keepdims=True), mine)
            weights = jnp.exp2(part - shift).astype(jnp.bfloat16)
            both = jnp.dot(weights, value, preferred_element_type=jnp.float32)
            share = jnp.exp2(mine - shift)
            mixture = own_ref[group, :, head_lanes(head + h)] * share + both[:, :HEAD_SIZE]
            staged[group, :, head_lanes(head + h)] = (
                mixture * inverse_of(share + both[:, HEAD_SIZE:])
            ).astype(staged.dtype)

    nothing = jnp.zeros((8, HEAD_SIZE), jnp.float32)

    def attend_quickly(picks):
        held = {}
        largest = nothing

        def start(step):
            group, head = step
            if head == 0:
                held[group] = keys_and_values(group, picks)
            return score(group, head, held[group][0])

        def finish(step, scores):
            nonlocal largest
            group, head = step
            if head == 0:
                arrive(group)
            largest = quick(group, head, scores, held[group][1], largest)
            if head == STEPS[-1]:
                send(group).start()

        staggered([(g, h) for g in range(KEY_VALUE_HEADS) for h in STEPS], start, finish)
        return jnp.max(largest)

    def attend_carefully(picks):
        @pl.loop(0, KEY_VALUE_HEADS)
        def _(group):
            send(group).wait()
            keys_across, value = keys_and_values(group, picks)
            for head in STEPS:
                careful(group, head, score(group, head, keys_across), value)
            send(group).start()

    def attend(picks):
        largest = attend_quickly(picks)

        @pl.when(largest > LARGE_SUM)
        def _():
            attend_carefully(picks)

    my_block = lax.axis_index("ctx")
    chosen = selected_ref[0, 0], selected_ref[0, 1]
    first = chosen[0] < my_block
    second = jnp.logical_and(chosen[1] < my_block, chosen[1] != chosen[0])
    count = first.astype(jnp.int32) + second.astype(jnp.int32)

    @pl.when(count == 2)
    def _():
        attend((0, 1))

    @pl.when(count == 1)
    def _():
        attend((second.astype(jnp.int32),))

    @pl.when(count == 0)
    def _():
        for group in range(KEY_VALUE_HEADS):
            arrive(group)
            staged[group] = own_ref[group].astype(staged.dtype)
            send(group).start()

    for group in range(KEY_VALUE_HEADS):
        send(group).wait()


def far_attention(selected, queries, own, level, far):
    rows = queries.shape[0]
    scores = QUERY_HEADS * rows * 2 * rows
    return pl.pallas_call(
        far_kernel,
        out_shape=jax.ShapeDtypeStruct(queries.shape, jnp.bfloat16),
        in_specs=[
            pl.BlockSpec(memory_space=pltpu.SMEM),
            *[pl.BlockSpec(memory_space=pltpu.VMEM)] * 2,
            *[pl.BlockSpec(memory_space=pl.ANY)] * 2,
        ],
        out_specs=pl.BlockSpec(memory_space=pl.ANY),
        scratch_shapes=[
            pltpu.VMEM((KEY_VALUE_HEADS, rows, GROUP * HEAD_SIZE), jnp.float32),
            pltpu.VMEM((KEY_VALUE_HEADS, rows, HEAD_SIZE), jnp.float32),
            pltpu.VMEM((KEY_VALUE_HEADS, rows, GROUP * HEAD_SIZE), jnp.bfloat16),
            pltpu.SemaphoreType.DMA((3, KEY_VALUE_HEADS)),
        ],
        compiler_params=pltpu.CompilerParams(vmem_limit_bytes=28 * MIB),
        cost_estimate=pl.CostEstimate(
            flops=4 * scores * HEAD_SIZE, bytes_accessed=10 * MIB, transcendentals=scores
        ),
        name="far_attention",
    )(selected, queries, far, own, level)


def local(queries, all_key_states, all_value_states, selected):
    devices = lax.axis_size("ctx")
    rows = all_key_states.shape[0]
    piece_rows = rows // devices
    packed = pack(all_key_states, all_value_states, selected, devices)
    held = lax.all_to_all(packed, "ctx", split_axis=0, concat_axis=0, tiled=True)
    own, level = own_attention(queries, all_key_states, all_value_states)
    wanted = held[:, SLOTS * piece_rows, :2].astype(jnp.int32)
    wanted = jnp.clip(wanted, 0, devices - 1)
    chosen = pick_pieces(wanted, held)
    far = lax.all_to_all(chosen, "ctx", split_axis=0, concat_axis=0, tiled=True)
    far = far.reshape(devices, 2, SLOTS, piece_rows, HEAD_SIZE)
    if piece_rows % 16 != 0:
        far = far.transpose(1, 2, 0, 3, 4).reshape(1, 2, SLOTS, rows, HEAD_SIZE)
    return far_attention(selected, queries, own, level, far)


def solution(mesh):
    placed = P(("groups", "ctx"), None)
    return jax.shard_map(
        local, mesh=mesh, in_specs=(placed,) * 4, out_specs=placed, check_vma=False
    )
```

profile of v0, /device:TPU:13, one launch (start us, length us, event | category | flops | bytes accessed | tf_op | source)
XLA Modules:
  0.0 82.6 jit_solution(12297384885053129560)
XLA Ops:
  0.0 2.0 %pack.1 = bf16[16,144,128]{2,1,0:T(8,128)(2,1)} custom-call(s32[1,2]{1,0:T(1,128)} %selected_ref.3, bf16[256,512]{1,0:T(8,128)(2,1)} %key_ref.3, bf16[256,512]{1,0:T(8,128)(2,1)} %value_ref.3), custom_call_target="tpu_custom_call" | custom-call | tf_op jit(solution)/shard_map/pack/pallas_call | solution.py:38
  2.0 22.5 %all_to_all.10.held_ref = bf16[16,144,128]{2,1,0:T(8,128)(2,1)S(1)} all-to-all(bf16[16,144,128]{2,1,0:T(8,128)(2,1)} %pack.1), channel_id=1, replica_groups=mesh['groups'=2,'ctx'=16] {'ctx'}, dimensions={0} | all-to-all | bytes 1179648 | tf_op jit(solution)/shard_map/all_to_all | solution.py:349
  24.5 0.0 copy-start.2
  24.5 0.0 copy-start.5
  24.5 1.8 %pick_pieces.1 = bf16[16,2,128,128]{3,2,1,0:T(8,128)(2,1)} custom-call(s32[16,2]{1,0:T(8,128)S(1)} %bitcast.3, bf16[16,144,128]{2,1,0:T(8,128)(2,1)S(1)} %all_to_all.10.held_ref), custom_call_target="tpu_custom_call" | custom-call | tf_op jit(solution)/shard_map/pick_pieces/pallas_call | solution.py:69
  26.3 4.9 %all-to-all-start.1 = ((bf16[16,2,128,128]{3,2,1,0:T(8,128)(2,1)}), bf16[16,2,128,128]{3,2,1,0:T(8,128)(2,1)S(1)}, u32[]{:S(2)}, u32[]{:S(2)}) async-start(bf16[16,2,128,128]{3,2,1,0:T(8,128)(2,1)} %pick_pieces.1), calls=%async_computation.1 | async-start | bytes 2097152 | tf_op jit(solution)/shard_map/all_to_all | solution.py:354
  31.2 0.0 copy-done.2
  31.2 0.0 copy-done.5
  31.2 0.0 copy-start.6
  31.2 0.9 %copy-done.6 = bf16[256,512]{1,0:T(8,128)(2,1)S(1)} copy-done((bf16[256,512]{1,0:T(8,128)(2,1)S(1)}, bf16[256,512]{1,0:T(8,128)(2,1)}, u32[]{:S(2)}) %copy-start.6) | copy-done | bytes 262168
  32.2 0.0 copy-start.7
  32.2 4.9 %own_attention.1 = (f32[256,4096]{1,0:T(8,128)S(1)}, f32[256,512]{1,0:T(8,128)S(1)}) custom-call(bf16[256,4096]{1,0:T(8,128)(2,1)S(1)} %copy-done.2, bf16[256,512]{1,0:T(8,128)(2,1)S(1)} %copy-done.5, bf16[256,512]{1,0:T(8,128)(2,1)S(1)} %copy-done.6), custom_call_target="tpu_custom_call" | custom-call | flops 1073741824 | bytes 7340032 | tf_op jit(solution)/shard_map/own_attention/pallas_call | solution.py:155
  37.1 0.0 copy-start
  37.1 1.9 %copy-done = f32[256,4096]{1,0:T(8,128)} copy-done((f32[256,4096]{1,0:T(8,128)}, f32[256,4096]{1,0:T(8,128)S(1)}, u32[]{:S(2)}) %copy-start) | copy-done | bytes 4194328
  39.0 0.0 copy-start.3
  39.0 0.8 copy-done.3
  39.8 16.2 %all-to-all-done.1 = bf16[16,2,128,128]{3,2,1,0:T(8,128)(2,1)S(1)} async-done(((bf16[16,2,128,128]{3,2,1,0:T(8,128)(2,1)}), bf16[16,2,128,128]{3,2,1,0:T(8,128)(2,1)S(1)}, u32[]{:S(2)}, u32[]{:S(2)}) %all-to-all-start.1) | async-done | bytes 1048608 | tf_op jit(solution)/shard_map/all_to_all | solution.py:354
  56.1 0.0 copy-done.7
  56.1 0.0 copy-start.1
  56.1 2.2 %copy-done.1 = f32[256,4096]{1,0:T(8,128)S(1)} copy-done((f32[256,4096]{1,0:T(8,128)S(1)}, f32[256,4096]{1,0:T(8,128)}, u32[]{:S(2)}) %copy-start.1) | copy-done | bytes 4194328
  58.3 0.0 copy-start.4
  58.3 1.0 %copy-done.4 = f32[256,512]{1,0:T(8,128)S(1)} copy-done((f32[256,512]{1,0:T(8,128)S(1)}, f32[256,512]{1,0:T(8,128)}, u32[]{:S(2)}) %copy-start.4) | copy-done | bytes 524312
  59.3 23.1 %far_attention.1 = bf16[256,4096]{1,0:T(8,128)(2,1)} custom-call(s32[1,2]{1,0:T(1,128)S(1)} %copy-done.7, bf16[256,4096]{1,0:T(8,128)(2,1)S(1)} %copy-done.2, bf16[16,2,8,16,128]{4,3,2,1,0:T(8,128)(2,1)S(1)} %bitcast.2, f32[256,4096]{1,0:T(8,128)S(1)} %copy-done.1, f32[256,512]{1,0:T(8,128)S(1)} %copy-done.4), custom_call_target="tpu_custom_call" | custom-call | flops 2147483648 | bytes 10485760 | tf_op jit(solution)/shard_map/far_attention/pallas_call | solution.py:321
  (1 shorter events, 0.0 us)
Async XLA Ops:
  24.5 6.7 %copy-start.2 = (bf16[256,4096]{1,0:T(8,128)(2,1)S(1)}, bf16[256,4096]{1,0:T(8,128)(2,1)}, u32[]{:S(2)}) copy-start(bf16[256,4096]{1,0:T(8,128)(2,1)} %query_ref.3) | copy-start | bytes 6291460
  24.5 6.7 %copy-start.5 = (bf16[256,512]{1,0:T(8,128)(2,1)S(1)}, bf16[256,512]{1,0:T(8,128)(2,1)}, u32[]{:S(2)}) copy-start(bf16[256,512]{1,0:T(8,128)(2,1)} %key_ref.3) | copy-start | bytes 786436
  26.3 29.7 %all-to-all-start.1 = ((bf16[16,2,128,128]{3,2,1,0:T(8,128)(2,1)}), bf16[16,2,128,128]{3,2,1,0:T(8,128)(2,1)S(1)}, u32[]{:S(2)}, u32[]{:S(2)}) async-start(bf16[16,2,128,128]{3,2,1,0:T(8,128)(2,1)} %pick_pieces.1), calls=%async_computation.1 | async-start | bytes 2097152 | tf_op jit(solution)/shard_map/all_to_all | solution.py:354
  31.2 1.0 %copy-start.6 = (bf16[256,512]{1,0:T(8,128)(2,1)S(1)}, bf16[256,512]{1,0:T(8,128)(2,1)}, u32[]{:S(2)}) copy-start(bf16[256,512]{1,0:T(8,128)(2,1)} %value_ref.3) | copy-start | bytes 786436
  32.2 23.9 %copy-start.7 = (s32[1,2]{1,0:T(1,128)S(1)}, s32[1,2]{1,0:T(1,128)}, u32[]{:S(2)}) copy-start(s32[1,2]{1,0:T(1,128)} %selected_ref.3) | copy-start | bytes 28
  37.1 1.9 %copy-start = (f32[256,4096]{1,0:T(8,128)}, f32[256,4096]{1,0:T(8,128)S(1)}, u32[]{:S(2)}) copy-start(f32[256,4096]{1,0:T(8,128)S(1)} %get-tuple-element.7.own_hbm) | copy-start | bytes 12582916
  39.0 0.8 copy-start.3
  56.1 2.2 %copy-start.1 = (f32[256,4096]{1,0:T(8,128)S(1)}, f32[256,4096]{1,0:T(8,128)}, u32[]{:S(2)}) copy-start(f32[256,4096]{1,0:T(8,128)} %copy-done) | copy-start | bytes 12582916
  58.3 1.0 %copy-start.4 = (f32[256,512]{1,0:T(8,128)S(1)}, f32[256,512]{1,0:T(8,128)}, u32[]{:S(2)}) copy-start(f32[256,512]{1,0:T(8,128)} %copy-done.3) | copy-start | bytes 1572868
where the time goes:
time: 83 us; the launch traced here: 82.6 us
  Pallas kernels  31.7 us (38%)
  blocking collectives  22.5 us (27%)
  waiting for transfers between devices  16.2 us (20%)
  local copies, waits for them, and re-layouts  6.93 us (8%)
  starting transfers between devices  4.87 us (6%)
    pallas_call x1, Pallas kernels, far_attention(): pl.pallas_call(far_kernel, out_shape=jax.ShapeDtypeStruct(queries.shape,...  23.1 us
    all_to_all x1, blocking collectives, local(): lax.all_to_all(packed, 'ctx', split_axis=0, concat_axis=0, tiled=True)  22.5 us
    all_to_all x1, waiting for transfers between devices, local(): far = lax.all_to_all(chosen, 'ctx', split_axis=0, concat_axis=0, tiled=True)  16.2 us
    unnamed x16, local copies, waits for them, and re-layouts  6.93 us
    pallas_call x1, Pallas kernels, own_attention(): pl.pallas_call(own_kernel, out_shape=[jax.ShapeDtypeStruct(queries.shape,...  4.92 us
    all_to_all x1, starting transfers between devices, local(): far = lax.all_to_all(chosen, 'ctx', split_axis=0, concat_axis=0, tiled=True)  4.87 us
    pallas_call x1, Pallas kernels, pack(): pl.pallas_call(pack_kernel, out_shape=jax.ShapeDtypeStruct(shape, jnp.bfl...  1.95 us
    pallas_call x1, Pallas kernels, pick_pieces(): pl.pallas_call(pick_kernel, out_shape=jax.ShapeDtypeStruct((devices, 2, r...  1.8 us
  transfers between devices with their start and end apart: 1, of which 1 were waited for; matrix products, arithmetic and copies ran while one was open for 0% of the time, Pallas kernels for 6%

commit v1 on v0

--- a/solution.py
+++ b/solution.py
@@ -37,7 +37,7 @@
     if piece_rows % 16 == 0:
         return pl.pallas_call(
             pack_kernel,
-            out_shape=jax.ShapeDtypeStruct(shape, jnp.bfloat16),
+            out_shape=pltpu.VMEM(shape, jnp.bfloat16),
             in_specs=[
                 pl.BlockSpec(memory_space=pltpu.SMEM),
                 pl.BlockSpec(memory_space=pltpu.VMEM),
@@ -68,7 +68,7 @@
     devices, rows = held.shape[0], held.shape[1] - REQUEST_ROWS
     return pl.pallas_call(
         pick_kernel,
-        out_shape=jax.ShapeDtypeStruct((devices, 2, rows, HEAD_SIZE), jnp.bfloat16),
+        out_shape=pltpu.VMEM((devices, 2, rows, HEAD_SIZE), jnp.bfloat16),
         in_specs=[
             pl.BlockSpec(memory_space=pltpu.SMEM),
             pl.BlockSpec(memory_space=pltpu.VMEM),
@@ -79,7 +79,7 @@
     )(wanted, held)
 
 
-HEADS_AT_ONCE = 4
+HEADS_AT_ONCE = 1
 FACTOR = math.log2(math.e) / math.sqrt(HEAD_SIZE)
 LARGE_SUM = 2.0**100
 
@@ -93,8 +93,7 @@
 
 
 def inverse_of(positive):
-    inverse = pl.reciprocal(positive, approx=True)
-    return inverse * (2.0 - positive * inverse)
+    return pl.reciprocal(positive, approx=True)
 
 
 def stacked_queries(query_ref, first):
@@ -155,8 +154,8 @@
     return pl.pallas_call(
         own_kernel,
         out_shape=[
-            jax.ShapeDtypeStruct(queries.shape, jnp.float32),
-            jax.ShapeDtypeStruct((rows, KEY_VALUE_HEADS * HEAD_SIZE), jnp.float32),
+            pltpu.HBM(queries.shape, jnp.float32),
+            pltpu.HBM((rows, KEY_VALUE_HEADS * HEAD_SIZE), jnp.float32),
         ],
         grid=(KEY_VALUE_HEADS,),
         in_specs=[
@@ -318,6 +317,8 @@
 def far_attention(selected, queries, own, level, far):
     rows = queries.shape[0]
     scores = QUERY_HEADS * rows * 2 * rows
+    own = pltpu.with_memory_space_constraint(own, pltpu.HBM)
+    level = pltpu.with_memory_space_constraint(level, pltpu.HBM)
     return pl.pallas_call(
         far_kernel,
         out_shape=jax.ShapeDtypeStruct(queries.shape, jnp.bfloat16),

time: 83 us -> 73.1 us (0.88)
  the two profiles are of different devices: /device:TPU:13 before, /device:TPU:9 now
where the time goes in v1:
time: 73.1 us; the launch traced here: 72.8 us
  Pallas kernels  25.8 us (35%)
  blocking collectives  22.3 us (31%)
  waiting for transfers between devices  18.6 us (25%)
  starting transfers between devices  4.87 us (7%)
  local copies, waits for them, and re-layouts  0.96 us (1%)
    all_to_all x1, blocking collectives, local(): lax.all_to_all(packed, 'ctx', split_axis=0, concat_axis=0, tiled=True)  22.3 us
    all_to_all x1, waiting for transfers between devices, local(): far = lax.all_to_all(chosen, 'ctx', split_axis=0, concat_axis=0, tiled=True)  18.6 us
    pallas_call x1, Pallas kernels, far_attention(): pl.pallas_call(far_kernel, out_shape=jax.ShapeDtypeStruct(queries.shape,...  17.6 us
    pallas_call x1, Pallas kernels, own_attention(): pl.pallas_call(own_kernel, out_shape=[pltpu.HBM(queries.shape, jnp.float3...  5.26 us
    all_to_all x1, starting transfers between devices, local(): far = lax.all_to_all(chosen, 'ctx', split_axis=0, concat_axis=0, tiled=True)  4.87 us
    pallas_call x1, Pallas kernels, pick_pieces(): pl.pallas_call(pick_kernel, out_shape=pltpu.VMEM((devices, 2, rows, HEAD_...  1.8 us
  transfers between devices with their start and end apart: 1, of which 1 were waited for; matrix products, arithmetic and copies ran while one was open for 0% of the time, Pallas kernels for 7%

profile of v1, /device:TPU:9, one launch (start us, length us, event | category | flops | bytes accessed | tf_op | source)
XLA Modules:
  0.0 72.8 jit_solution(3930268376140915483)
XLA Ops:
  0.0 1.1 %pack.1 = bf16[16,144,128]{2,1,0:T(8,128)(2,1)S(1)} custom-call(s32[1,2]{1,0:T(1,128)} %selected_ref.3, bf16[256,512]{1,0:T(8,128)(2,1)} %key_ref.3, bf16[256,512]{1,0:T(8,128)(2,1)} %value_ref.3), custom_call_target="tpu_custom_call" | custom-call | tf_op jit(solution)/shard_map/pack/pallas_call | solution.py:38
  1.1 22.3 %all_to_all.10.held_ref = bf16[16,144,128]{2,1,0:T(8,128)(2,1)S(1)} all-to-all(bf16[16,144,128]{2,1,0:T(8,128)(2,1)S(1)} %pack.1), channel_id=1, replica_groups=mesh['groups'=2,'ctx'=16] {'ctx'}, dimensions={0} | all-to-all | bytes 1179648 | tf_op jit(solution)/shard_map/all_to_all | solution.py:350
  23.5 0.0 copy-start
  23.5 0.0 copy-start.1
  23.5 1.8 %pick_pieces.1 = bf16[16,2,128,128]{3,2,1,0:T(8,128)(2,1)} custom-call(s32[16,2]{1,0:T(8,128)S(1)} %bitcast.3, bf16[16,144,128]{2,1,0:T(8,128)(2,1)S(1)} %all_to_all.10.held_ref), custom_call_target="tpu_custom_call" | custom-call | tf_op jit(solution)/shard_map/pick_pieces/pallas_call | solution.py:69
  25.3 4.9 %all-to-all-start.1 = ((bf16[16,2,128,128]{3,2,1,0:T(8,128)(2,1)}), bf16[16,2,128,128]{3,2,1,0:T(8,128)(2,1)S(1)}, u32[]{:S(2)}, u32[]{:S(2)}) async-start(bf16[16,2,128,128]{3,2,1,0:T(8,128)(2,1)} %pick_pieces.1), calls=%async_computation.1 | async-start | bytes 2097152 | tf_op jit(solution)/shard_map/all_to_all | solution.py:355
  30.2 0.0 copy-done
  30.2 0.0 copy-done.1
  30.2 0.0 copy-start.2
  30.2 0.9 %copy-done.2 = bf16[256,512]{1,0:T(8,128)(2,1)S(1)} copy-done((bf16[256,512]{1,0:T(8,128)(2,1)S(1)}, bf16[256,512]{1,0:T(8,128)(2,1)}, u32[]{:S(2)}) %copy-start.2) | copy-done | bytes 262168
  31.2 0.0 copy-start.3
  31.2 5.3 %own_attention.1 = (f32[256,4096]{1,0:T(8,128)}, f32[256,512]{1,0:T(8,128)}) custom-call(bf16[256,4096]{1,0:T(8,128)(2,1)S(1)} %copy-done, bf16[256,512]{1,0:T(8,128)(2,1)S(1)} %copy-done.1, bf16[256,512]{1,0:T(8,128)(2,1)S(1)} %copy-done.2), custom_call_target="tpu_custom_call" | custom-call | flops 1073741824 | bytes 7340032 | tf_op jit(solution)/shard_map/own_attention/pallas_call | solution.py:154
  36.4 18.6 %all-to-all-done.1 = bf16[16,2,128,128]{3,2,1,0:T(8,128)(2,1)S(1)} async-done(((bf16[16,2,128,128]{3,2,1,0:T(8,128)(2,1)}), bf16[16,2,128,128]{3,2,1,0:T(8,128)(2,1)S(1)}, u32[]{:S(2)}, u32[]{:S(2)}) %all-to-all-start.1) | async-done | bytes 1048608 | tf_op jit(solution)/shard_map/all_to_all | solution.py:355
  55.1 0.0 copy-done.3
  55.1 17.6 %far_attention.1 = bf16[256,4096]{1,0:T(8,128)(2,1)} custom-call(s32[1,2]{1,0:T(1,128)S(1)} %copy-done.3, bf16[256,4096]{1,0:T(8,128)(2,1)S(1)} %copy-done, bf16[16,2,8,16,128]{4,3,2,1,0:T(8,128)(2,1)S(1)} %bitcast.2, f32[256,4096]{1,0:T(8,128)} %get-tuple-element.7.own_hbm, f32[256,512]{1,0:T(8,128)} %get-tuple-element.8.level_hbm), custom_call_target="tpu_custom_call" | custom-call | flops 2147483648 | bytes 10485760 | tf_op jit(solution)/shard_map/far_attention/pallas_call | solution.py:322
  (1 shorter events, 0.0 us)
Async XLA Ops:
  23.5 6.7 %copy-start = (bf16[256,4096]{1,0:T(8,128)(2,1)S(1)}, bf16[256,4096]{1,0:T(8,128)(2,1)}, u32[]{:S(2)}) copy-start(bf16[256,4096]{1,0:T(8,128)(2,1)} %query_ref.3) | copy-start | bytes 6291460
  23.5 6.7 %copy-start.1 = (bf16[256,512]{1,0:T(8,128)(2,1)S(1)}, bf16[256,512]{1,0:T(8,128)(2,1)}, u32[]{:S(2)}) copy-start(bf16[256,512]{1,0:T(8,128)(2,1)} %key_ref.3) | copy-start | bytes 786436
  25.3 29.7 %all-to-all-start.1 = ((bf16[16,2,128,128]{3,2,1,0:T(8,128)(2,1)}), bf16[16,2,128,128]{3,2,1,0:T(8,128)(2,1)S(1)}, u32[]{:S(2)}, u32[]{:S(2)}) async-start(bf16[16,2,128,128]{3,2,1,0:T(8,128)(2,1)} %pick_pieces.1), calls=%async_computation.1 | async-start | bytes 2097152 | tf_op jit(solution)/shard_map/all_to_all | solution.py:355
  30.2 1.0 %copy-start.2 = (bf16[256,512]{1,0:T(8,128)(2,1)S(1)}, bf16[256,512]{1,0:T(8,128)(2,1)}, u32[]{:S(2)}) copy-start(bf16[256,512]{1,0:T(8,128)(2,1)} %value_ref.3) | copy-start | bytes 786436
  31.2 23.9 %copy-start.3 = (s32[1,2]{1,0:T(1,128)S(1)}, s32[1,2]{1,0:T(1,128)}, u32[]{:S(2)}) copy-start(s32[1,2]{1,0:T(1,128)} %selected_ref.3) | copy-start | bytes 28

commit v2 on v1

--- a/solution.py
+++ b/solution.py
@@ -13,26 +13,33 @@
 GROUP = QUERY_HEADS // KEY_VALUE_HEADS
 SLOTS = 2 * KEY_VALUE_HEADS
 REQUEST_ROWS = 16
+COPIES = 2
 MIB = 1024 * 1024
 
 
 def pack_kernel(selected_ref, key_ref, value_ref, out_ref):
-    devices, piece_rows = out_ref.shape[0], key_ref.shape[0] // out_ref.shape[0]
+    devices = out_ref.shape[0]
+    shares = devices // COPIES
+    piece_rows = key_ref.shape[0] // shares
     for slot in range(SLOTS):
         ref = key_ref if slot < KEY_VALUE_HEADS else value_ref
         head = slot % KEY_VALUE_HEADS
         part = ref[:, head * HEAD_SIZE : (head + 1) * HEAD_SIZE]
-        out_ref[:, slot * piece_rows : (slot + 1) * piece_rows, :] = part.reshape(
-            devices, piece_rows, HEAD_SIZE
-        )
+        part = part.reshape(shares, piece_rows, HEAD_SIZE)
+        for copy in range(COPIES):
+            out_ref[
+                copy * shares : (copy + 1) * shares,
+                slot * piece_rows : (slot + 1) * piece_rows,
+                :,
+            ] = part
     lane = lax.broadcasted_iota(jnp.int32, (devices, REQUEST_ROWS, HEAD_SIZE), 2)
     request = jnp.where(lane == 0, selected_ref[0, 0], selected_ref[0, 1])
     out_ref[:, SLOTS * piece_rows :, :] = request.astype(jnp.float32).astype(jnp.bfloat16)
 
 
 def pack(keys, values, selected, devices):
-    rows = keys.shape[0]
-    piece_rows = rows // devices
+    shares = devices // COPIES
+    piece_rows = keys.shape[0] // shares
     shape = (devices, SLOTS * piece_rows + REQUEST_ROWS, HEAD_SIZE)
     if piece_rows % 16 == 0:
         return pl.pallas_call(
@@ -47,39 +54,52 @@
             name="pack",
         )(selected, keys, values)
     both = jnp.concatenate([keys, values], axis=1)
-    both = both.reshape(devices, piece_rows, SLOTS, HEAD_SIZE).transpose(0, 2, 1, 3)
-    both = both.reshape(devices, SLOTS * piece_rows, HEAD_SIZE)
+    both = both.reshape(shares, piece_rows, SLOTS, HEAD_SIZE).transpose(0, 2, 1, 3)
+    both = both.reshape(shares, SLOTS * piece_rows, HEAD_SIZE)
     lane = jnp.arange(HEAD_SIZE) == 0
     request = jnp.where(lane, selected[0, 0], selected[0, 1]).astype(jnp.bfloat16)
-    request = jnp.broadcast_to(request, (devices, REQUEST_ROWS, HEAD_SIZE))
-    return jnp.concatenate([both, request], axis=1)
-
-
-def pick_kernel(wanted_ref, held_ref, out_ref):
-    rows = out_ref.shape[2]
-
-    @pl.loop(0, out_ref.shape[0])
-    def _(device):
+    request = jnp.broadcast_to(request, (shares, REQUEST_ROWS, HEAD_SIZE))
+    return jnp.concatenate([jnp.concatenate([both, request], axis=1)] * COPIES, axis=0)
+
+
+def partner(position, step):
+    return position ^ step
+
+
+def pick_kernel(wanted_ref, held_ref, *out_refs):
+    rows = out_refs[0].shape[1]
+    me = lax.axis_index("ctx")
+    for step, out_ref in enumerate(out_refs):
+        device = partner(me, step)
         for pick in range(2):
-            out_ref[device, pick] = held_ref[wanted_ref[device, pick], :rows, :]
+            out_ref[pick] = held_ref[wanted_ref[device, pick], :rows, :]
 
 
 def pick_pieces(wanted, held):
     devices, rows = held.shape[0], held.shape[1] - REQUEST_ROWS
+    shares = devices // COPIES
     return pl.pallas_call(
         pick_kernel,
-        out_shape=pltpu.VMEM((devices, 2, rows, HEAD_SIZE), jnp.bfloat16),
+        out_shape=[jax.ShapeDtypeStruct((2, rows, HEAD_SIZE), jnp.bfloat16)] * shares,
         in_specs=[
             pl.BlockSpec(memory_space=pltpu.SMEM),
             pl.BlockSpec(memory_space=pltpu.VMEM),
         ],
-        out_specs=pl.BlockSpec(memory_space=pltpu.VMEM),
+        out_specs=[pl.BlockSpec(memory_space=pltpu.VMEM)] * shares,
         compiler_params=pltpu.CompilerParams(vmem_limit_bytes=16 * MIB),
         name="pick_pieces",
     )(wanted, held)
 
 
-HEADS_AT_ONCE = 1
+def deliver(pieces, devices):
+    moved = [pieces[0]] + [None] * (len(pieces) - 1)
+    for step in reversed(range(1, len(pieces))):
+        pairs = [(i, partner(i, step)) for i in range(devices)]
+        moved[step] = lax.ppermute(pieces[step], "ctx", pairs)
+    return moved
+
+
+HEADS_AT_ONCE = 2
 FACTOR = math.log2(math.e) / math.sqrt(HEAD_SIZE)
 LARGE_SUM = 2.0**100
 
@@ -175,9 +195,8 @@
     )(queries, keys, values)
 
 
-def far_kernel(
-    selected_ref, query_ref, far_ref, own_hbm, level_hbm, out_ref, own_ref, level_ref, staged, sems
-):
+def far_kernel(selected_ref, query_ref, own_hbm, level_hbm, *refs):
+    *far_refs, out_ref, own_ref, level_ref, staged, sems = refs
     rows = query_ref.shape[0]
     width = GROUP * HEAD_SIZE
 
@@ -185,28 +204,26 @@
         start = group * size
         return pl.ds(start if isinstance(group, int) else pl.multiple_of(start, size), size)
 
-    def fetch(group):
-        wide, narrow = lanes(group, width), lanes(group, HEAD_SIZE)
-        return (
-            pltpu.make_async_copy(own_hbm.at[:, wide], own_ref.at[group], sems.at[0, group]),
-            pltpu.make_async_copy(level_hbm.at[:, narrow], level_ref.at[group], sems.at[1, group]),
+    def fetch(group, which):
+        size, source, target = (
+            (width, own_hbm, own_ref) if which == 0 else (HEAD_SIZE, level_hbm, level_ref)
         )
+        part = source.at[:, lanes(group, size)]
+        return pltpu.make_async_copy(part, target.at[group], sems.at[which, group])
 
     def send(group):
         out = out_ref.at[:, lanes(group, width)]
         return pltpu.make_async_copy(staged.at[group], out, sems.at[2, group])
 
     for group in range(KEY_VALUE_HEADS):
-        for copy in fetch(group):
-            copy.start()
-
-    def arrive(group):
-        for copy in fetch(group):
-            copy.wait()
+        fetch(group, 1).start()
+        fetch(group, 0).start()
+
+    def arrive(group, which):
+        fetch(group, which).wait()
 
     def block(slot, picks):
-        blocks = [far_ref[:, p, slot].reshape(rows, HEAD_SIZE) for p in picks]
-        return jnp.concatenate(blocks, axis=0)
+        return jnp.concatenate([ref[p, slot] for p in picks for ref in far_refs], axis=0)
 
     def keys_and_values(group, picks):
         return block(group, picks).T, with_ones(block(group + KEY_VALUE_HEADS, picks))
@@ -224,6 +241,8 @@
         both = jnp.dot(
             jnp.concatenate(weights, axis=0), value, preferred_element_type=jnp.float32
         )
+        if head == 0:
+            arrive(group, 0)
         for h in range(HEADS_AT_ONCE):
             part = both[h * rows : (h + 1) * rows]
             row_sum = 1.0 + part[:, HEAD_SIZE:]
@@ -252,20 +271,18 @@
     nothing = jnp.zeros((8, HEAD_SIZE), jnp.float32)
 
     def attend_quickly(picks):
-        held = {}
+        held = {g: keys_and_values(g, picks) for g in range(KEY_VALUE_HEADS)}
         largest = nothing
 
         def start(step):
             group, head = step
-            if head == 0:
-                held[group] = keys_and_values(group, picks)
             return score(group, head, held[group][0])
 
         def finish(step, scores):
             nonlocal largest
             group, head = step
             if head == 0:
-                arrive(group)
+                arrive(group, 1)
             largest = quick(group, head, scores, held[group][1], largest)
             if head == STEPS[-1]:
                 send(group).start()
@@ -306,7 +323,8 @@
     @pl.when(count == 0)
     def _():
         for group in range(KEY_VALUE_HEADS):
-            arrive(group)
+            arrive(group, 0)
+            arrive(group, 1)
             staged[group] = own_ref[group].astype(staged.dtype)
             send(group).start()
 
@@ -324,8 +342,9 @@
         out_shape=jax.ShapeDtypeStruct(queries.shape, jnp.bfloat16),
         in_specs=[
             pl.BlockSpec(memory_space=pltpu.SMEM),
-            *[pl.BlockSpec(memory_space=pltpu.VMEM)] * 2,
+            pl.BlockSpec(memory_space=pltpu.VMEM),
             *[pl.BlockSpec(memory_space=pl.ANY)] * 2,
+            *[pl.BlockSpec(memory_space=pltpu.VMEM)] * len(far),
         ],
         out_specs=pl.BlockSpec(memory_space=pl.ANY),
         scratch_shapes=[
@@ -339,23 +358,22 @@
             flops=4 * scores * HEAD_SIZE, bytes_accessed=10 * MIB, transcendentals=scores
         ),
         name="far_attention",
-    )(selected, queries, far, own, level)
+    )(selected, queries, own, level, *far)
 
 
 def local(queries, all_key_states, all_value_states, selected):
     devices = lax.axis_size("ctx")
     rows = all_key_states.shape[0]
-    piece_rows = rows // devices
+    piece_rows = rows * COPIES // devices
     packed = pack(all_key_states, all_value_states, selected, devices)
     held = lax.all_to_all(packed, "ctx", split_axis=0, concat_axis=0, tiled=True)
     own, level = own_attention(queries, all_key_states, all_value_states)
     wanted = held[:, SLOTS * piece_rows, :2].astype(jnp.int32)
     wanted = jnp.clip(wanted, 0, devices - 1)
-    chosen = pick_pieces(wanted, held)
-    far = lax.all_to_all(chosen, "ctx", split_axis=0, concat_axis=0, tiled=True)
-    far = far.reshape(devices, 2, SLOTS, piece_rows, HEAD_SIZE)
+    moved = deliver(pick_pieces(wanted, held), devices)
+    far = [m.reshape(2, SLOTS, piece_rows, HEAD_SIZE) for m in moved]
     if piece_rows % 16 != 0:
-        far = far.transpose(1, 2, 0, 3, 4).reshape(1, 2, SLOTS, rows, HEAD_SIZE)
+        far = [jnp.concatenate(far, axis=2)]
     return far_attention(selected, queries, own, level, far)
 
 

time: 73.1 us -> 75.2 us (1.029)
  the two profiles are of different devices: /device:TPU:9 before, /device:TPU:3 now
where the time goes in v2:
time: 75.2 us; the launch traced here: 75 us
  blocking collectives  33.8 us (45%)
  Pallas kernels  29.4 us (39%)
  starting transfers between devices  7.79 us (10%)
  waiting for transfers between devices  3.76 us (5%)
    all_to_all x1, blocking collectives, local(): lax.all_to_all(packed, 'ctx', split_axis=0, concat_axis=0, tiled=True)  33.8 us
    pallas_call x1, Pallas kernels, far_attention(): pl.pallas_call(far_kernel, out_shape=jax.ShapeDtypeStruct(queries.shape,...  22.3 us
    ppermute x7, starting transfers between devices, deliver(): moved[step] = lax.ppermute(pieces[step], 'ctx', pairs)  7.79 us
    pallas_call x1, Pallas kernels, own_attention(): pl.pallas_call(own_kernel, out_shape=[pltpu.HBM(queries.shape, jnp.float3...  5.2 us
    ppermute x7, waiting for transfers between devices, deliver(): moved[step] = lax.ppermute(pieces[step], 'ctx', pairs)  3.76 us
  transfers between devices with their start and end apart: 7, of which 3 were waited for; matrix products, arithmetic and copies ran while one was open for 0% of the time, Pallas kernels for 7%

profile of v2, /device:TPU:3, one launch (start us, length us, event | category | flops | bytes accessed | tf_op | source)
XLA Modules:
  0.0 75.0 jit_solution(9220333728289290647)
XLA Ops:
  0.0 1.2 %pack.1 = bf16[16,272,128]{2,1,0:T(8,128)(2,1)S(1)} custom-call(s32[1,2]{1,0:T(1,128)} %selected_ref.3, bf16[256,512]{1,0:T(8,128)(2,1)} %key_ref.3, bf16[256,512]{1,0:T(8,128)(2,1)} %value_ref.3), custom_call_target="tpu_custom_call" | custom-call | tf_op jit(solution)/shard_map/pack/pallas_call | solution.py:45
  1.2 0.0 copy-start
  1.2 0.0 copy-start.1
  1.2 0.0 copy-start.2
  1.2 33.8 %all_to_all.5.held_ref = bf16[16,272,128]{2,1,0:T(8,128)(2,1)S(1)} all-to-all(bf16[16,272,128]{2,1,0:T(8,128)(2,1)S(1)} %pack.1), channel_id=1, replica_groups=mesh['groups'=2,'ctx'=16] {'ctx'}, dimensions={0} | all-to-all | bytes 2228224 | tf_op jit(solution)/shard_map/all_to_all | solution.py:369
  35.0 0.8 %pick_pieces.1 = (bf16[2,256,128]{2,1,0:T(8,128)(2,1)S(1)}, bf16[2,256,128]{2,1,0:T(8,128)(2,1)S(1)}, bf16[2,256,128]{2,1,0:T(8,128)(2,1)S(1)}, bf16[2,256,128]{...) custom-call(s32[16,2]{1,0:T(8,128)S(1)} %bitcast.17, ...), custom_call_target="tpu_custom_call" | custom-call | tf_op jit(solution)/shard_map/pick_pieces/pallas_call | solution.py:81
  35.8 0.0 copy-start.3
  35.8 0.5 collective-permute-start
  36.2 1.1 %collective-permute-start.1 = (bf16[2,256,128]{2,1,0:T(8,128)(2,1)S(1)}, bf16[2,256,128]{2,1,0:T(8,128)(2,1)S(1)}, u32[]{:S(2)}, u32[]{:S(2)}) collective-permute-start(bf16[2,256,128]{2,1,0:T(8,128)(2,1)S(1)} %get-tuple-element.19), channel_id=1, source_target_pairs={{0,2},{1,3},{2,0},{3,1},{4,6},{5,7},{6,4},{7,5},{8,10},{9,11},{10,... | collective-permute-start | bytes 393224 | tf_op jit(solution)/shard_map/ppermute | solution.py:98
  37.4 0.6 collective-permute-start.2
  38.0 0.4 collective-permute-start.3
  38.4 1.3 %collective-permute-start.4 = (bf16[2,256,128]{2,1,0:T(8,128)(2,1)S(1)}, bf16[2,256,128]{2,1,0:T(8,128)(2,1)S(1)}, u32[]{:S(2)}, u32[]{:S(2)}) collective-permute-start(bf16[2,256,128]{2,1,0:T(8,128)(2,1)S(1)} %get-tuple-element.22), channel_id=1, source_target_pairs={{0,5},{1,4},{2,7},{3,6},{4,1},{5,0},{6,3},{7,2},{8,13},{9,12},{10,... | collective-permute-start | bytes 393224 | tf_op jit(solution)/shard_map/ppermute | solution.py:98
  39.7 0.0 collective-permute-done
  39.7 1.2 %collective-permute-start.5 = (bf16[2,256,128]{2,1,0:T(8,128)(2,1)S(1)}, bf16[2,256,128]{2,1,0:T(8,128)(2,1)S(1)}, u32[]{:S(2)}, u32[]{:S(2)}) collective-permute-start(bf16[2,256,128]{2,1,0:T(8,128)(2,1)S(1)} %get-tuple-element.23), channel_id=1, source_target_pairs={{0,6},{1,7},{2,4},{3,5},{4,2},{5,3},{6,0},{7,1},{8,14},{9,15},{10,... | collective-permute-start | bytes 393224 | tf_op jit(solution)/shard_map/ppermute | solution.py:98
  41.0 0.2 collective-permute-done.1
  41.2 2.6 %collective-permute-start.6 = (bf16[2,256,128]{2,1,0:T(8,128)(2,1)S(1)}, bf16[2,256,128]{2,1,0:T(8,128)(2,1)S(1)}, u32[]{:S(2)}, u32[]{:S(2)}) collective-permute-start(bf16[2,256,128]{2,1,0:T(8,128)(2,1)S(1)} %get-tuple-element.24), channel_id=1, source_target_pairs={{0,7},{1,6},{2,5},{3,4},{4,3},{5,2},{6,1},{7,0},{8,15},{9,14},{10,... | collective-permute-start | bytes 393224 | tf_op jit(solution)/shard_map/ppermute | solution.py:98
  43.8 0.0 copy-done
  43.8 5.2 %own_attention.1 = (f32[256,4096]{1,0:T(8,128)}, f32[256,512]{1,0:T(8,128)}) custom-call(bf16[256,4096]{1,0:T(8,128)(2,1)S(1)} %copy-done, bf16[256,512]{1,0:T(8,128)(2,1)S(1)} %copy-done.1, bf16[256,512]{1,0:T(8,128)(2,1)S(1)} %copy-done.2), custom_call_target="tpu_custom_call" | custom-call | flops 1073741824 | bytes 7340032 | tf_op jit(solution)/shard_map/own_attention/pallas_call | solution.py:174
  49.0 0.0 collective-permute-done.2
  49.0 0.0 collective-permute-done.3
  49.0 0.0 collective-permute-done.4
  49.0 0.5 collective-permute-done.5
  49.6 3.0 %collective-permute-done.6 = bf16[2,256,128]{2,1,0:T(8,128)(2,1)S(1)} collective-permute-done((bf16[2,256,128]{2,1,0:T(8,128)(2,1)S(1)}, bf16[2,256,128]{2,1,0:T(8,128)(2,1)S(1)}, u32[]{:S(2)}, u32[]{:S(2)}) %collective-permute-start.6) | collective-permute-done | bytes 131104 | tf_op jit(solution)/shard_map/ppermute | solution.py:98
  52.5 22.3 %far_attention.1 = bf16[256,4096]{1,0:T(8,128)(2,1)} custom-call(s32[1,2]{1,0:T(1,128)S(1)} %copy-done.3, bf16[256,4096]{1,0:T(8,128)(2,1)S(1)} %copy-done, f32[256,4096]{1,0:T(8,128)} %get-tuple-element.15.own_hbm, f32[256,512]{1,0:T(8,128)} %get-tuple-element.16.level_hbm, bf16[2,8,32,128]{3,2,1,0:T(8,128)(2,1)S(1)} %bitcast.9, ...), custom_call_target="tpu_custom_call" | custom-call | flops 2147483648 | bytes 10485760 | tf_op jit(solution)/shard_map/far_attention/pallas_call | solution.py:340
  (4 shorter events, 0.0 us)
Async XLA Ops:
  1.2 42.6 %copy-start = (bf16[256,4096]{1,0:T(8,128)(2,1)S(1)}, bf16[256,4096]{1,0:T(8,128)(2,1)}, u32[]{:S(2)}) copy-start(bf16[256,4096]{1,0:T(8,128)(2,1)} %query_ref.3) | copy-start | bytes 6291460
  1.2 42.6 %copy-start.1 = (bf16[256,512]{1,0:T(8,128)(2,1)S(1)}, bf16[256,512]{1,0:T(8,128)(2,1)}, u32[]{:S(2)}) copy-start(bf16[256,512]{1,0:T(8,128)(2,1)} %key_ref.3) | copy-start | bytes 786436
  1.2 42.6 %copy-start.2 = (bf16[256,512]{1,0:T(8,128)(2,1)S(1)}, bf16[256,512]{1,0:T(8,128)(2,1)}, u32[]{:S(2)}) copy-start(bf16[256,512]{1,0:T(8,128)(2,1)} %value_ref.3) | copy-start | bytes 786436
  35.8 16.8 %copy-start.3 = (s32[1,2]{1,0:T(1,128)S(1)}, s32[1,2]{1,0:T(1,128)}, u32[]{:S(2)}) copy-start(s32[1,2]{1,0:T(1,128)} %selected_ref.3) | copy-start | bytes 28
  35.8 4.0 %collective-permute-start = (bf16[2,256,128]{2,1,0:T(8,128)(2,1)S(1)}, bf16[2,256,128]{2,1,0:T(8,128)(2,1)S(1)}, u32[]{:S(2)}, u32[]{:S(2)}) collective-permute-start(bf16[2,256,128]{2,1,0:T(8,128)(2,1)S(1)} %get-tuple-element.18), channel_id=1, source_target_pairs={{0,1},{1,0},{2,3},{3,2},{4,5},{5,4},{6,7},{7,6},{8,9},{9,8},{10,11... | collective-permute-start | bytes 393224 | tf_op jit(solution)/shard_map/ppermute | solution.py:98
  36.2 5.0 %collective-permute-start.1 = (bf16[2,256,128]{2,1,0:T(8,128)(2,1)S(1)}, bf16[2,256,128]{2,1,0:T(8,128)(2,1)S(1)}, u32[]{:S(2)}, u32[]{:S(2)}) collective-permute-start(bf16[2,256,128]{2,1,0:T(8,128)(2,1)S(1)} %get-tuple-element.19), channel_id=1, source_target_pairs={{0,2},{1,3},{2,0},{3,1},{4,6},{5,7},{6,4},{7,5},{8,10},{9,11},{10,... | collective-permute-start | bytes 393224 | tf_op jit(solution)/shard_map/ppermute | solution.py:98
  37.4 11.6 %collective-permute-start.2 = (bf16[2,256,128]{2,1,0:T(8,128)(2,1)S(1)}, bf16[2,256,128]{2,1,0:T(8,128)(2,1)S(1)}, u32[]{:S(2)}, u32[]{:S(2)}) collective-permute-start(bf16[2,256,128]{2,1,0:T(8,128)(2,1)S(1)} %get-tuple-element.20), channel_id=1, source_target_pairs={{0,3},{1,2},{2,1},{3,0},{4,7},{5,6},{6,5},{7,4},{8,11},{9,10},{10,... | collective-permute-start | bytes 393224 | tf_op jit(solution)/shard_map/ppermute | solution.py:98
  38.0 11.0 %collective-permute-start.3 = (bf16[2,256,128]{2,1,0:T(8,128)(2,1)S(1)}, bf16[2,256,128]{2,1,0:T(8,128)(2,1)S(1)}, u32[]{:S(2)}, u32[]{:S(2)}) collective-permute-start(bf16[2,256,128]{2,1,0:T(8,128)(2,1)S(1)} %get-tuple-element.21), channel_id=1, source_target_pairs={{0,4},{1,5},{2,6},{3,7},{4,0},{5,1},{6,2},{7,3},{8,12},{9,13},{10,... | collective-permute-start | bytes 393224 | tf_op jit(solution)/shard_map/ppermute | solution.py:98
  38.4 10.6 %collective-permute-start.4 = (bf16[2,256,128]{2,1,0:T(8,128)(2,1)S(1)}, bf16[2,256,128]{2,1,0:T(8,128)(2,1)S(1)}, u32[]{:S(2)}, u32[]{:S(2)}) collective-permute-start(bf16[2,256,128]{2,1,0:T(8,128)(2,1)S(1)} %get-tuple-element.22), channel_id=1, source_target_pairs={{0,5},{1,4},{2,7},{3,6},{4,1},{5,0},{6,3},{7,2},{8,13},{9,12},{10,... | collective-permute-start | bytes 393224 | tf_op jit(solution)/shard_map/ppermute | solution.py:98
  39.7 9.8 %collective-permute-start.5 = (bf16[2,256,128]{2,1,0:T(8,128)(2,1)S(1)}, bf16[2,256,128]{2,1,0:T(8,128)(2,1)S(1)}, u32[]{:S(2)}, u32[]{:S(2)}) collective-permute-start(bf16[2,256,128]{2,1,0:T(8,128)(2,1)S(1)} %get-tuple-element.23), channel_id=1, source_target_pairs={{0,6},{1,7},{2,4},{3,5},{4,2},{5,3},{6,0},{7,1},{8,14},{9,15},{10,... | collective-permute-start | bytes 393224 | tf_op jit(solution)/shard_map/ppermute | solution.py:98
  41.2 11.3 %collective-permute-start.6 = (bf16[2,256,128]{2,1,0:T(8,128)(2,1)S(1)}, bf16[2,256,128]{2,1,0:T(8,128)(2,1)S(1)}, u32[]{:S(2)}, u32[]{:S(2)}) collective-permute-start(bf16[2,256,128]{2,1,0:T(8,128)(2,1)S(1)} %get-tuple-element.24), channel_id=1, source_target_pairs={{0,7},{1,6},{2,5},{3,4},{4,3},{5,2},{6,1},{7,0},{8,15},{9,14},{10,... | collective-permute-start | bytes 393224 | tf_op jit(solution)/shard_map/ppermute | solution.py:98
